TPU v7x, 32 devices: a whole 2x2x4 slice. The times are simulated.
32 devices in a mesh: parts: 2 (over x), row: 16 (over z, y, core).
Axes of the slice: x: 2, y: 2, z: 4, core: 2. Of those that a mesh axis runs over, the one named last changes fastest.
Arguments:
- basis_values: float32 [32768, 512], P(('parts', 'row')), parts along dimension 0, may hold values from 0.01 to 0.1
- basis_grads: float32 [3, 32768, 512], P(None, ('parts', 'row')), parts along dimension 1, may hold values from -6 to 6
- weights: float32 [32768], P(('parts', 'row')), parts along dimension 0, may hold values from 0.2 to 2
- tile_lists: int32 [32, 8], P('parts'), parts along dimension 0, may hold values from 0 to 15, as said below
- tile_counts: int32 [32], P('parts'), parts along dimension 0, may hold values from 7 to 8, as said below
- owned_rows: int32 [32], P('parts'), parts along dimension 0, may hold values from 0 to 15, as said below
- density_slabs: float32 [2048, 1024], P(('parts', 'row')), parts along dimension 0, as said below
Outputs:
- potential_slabs: float32 [2048, 1024], P(('parts', 'row')), parts along dimension 0
There are 2 independent parts, one for each index of `parts`. A program takes and returns all parts, laid end to end along the dimension named above; each array names one. Nothing has to cross between parts.
Inputs may be any that keep to these rules, and one draw needn't show every extreme that they name: `tile_lists`: each row lists 8 distinct tile indices. `tile_counts`: some batch has all 8 slots significant. `owned_rows`: a permutation of the tile rows. `density_slabs`: the matrix P assembled from the blocks is symmetric, with positive entries.
All inputs are finite; a program needn't handle non-finite values.
Results may differ from a plain program's by a relative error of at most 0.0003.
Values sent between devices are 32-bit elements; how exact they have to be, the bound alone decides.
A program may use at most 128 MiB of HBM per device.

v0:
```python
import math

import jax
import jax.numpy as jnp
from jax import lax
from jax.sharding import PartitionSpec as P

KAPPA = 0.804
MU_COEF = 0.2195


def energy_density(rho, sigma):
    coef = 0.75 * (3.0 / math.pi) ** (1.0 / 3.0)
    scale = 4.0 * (3.0 * math.pi**2) ** (2.0 / 3.0)
    reduced = sigma / (scale * jnp.power(rho, 8.0 / 3.0))
    factor = 1.0 + KAPPA - KAPPA / (1.0 + MU_COEF * reduced / KAPPA)
    return -coef * jnp.power(rho, 4.0 / 3.0) * factor


def pbe_block(values, grads, wts, dens):
    highest = lax.Precision.HIGHEST
    mixed = jnp.dot(values, dens, precision=highest, preferred_element_type=jnp.float32)
    rho = jnp.sum(mixed * values, axis=1)
    slope = 2.0 * jnp.sum(mixed[None, :, :] * grads, axis=2)
    sigma = jnp.sum(slope * slope, axis=0)
    energy, pull = jax.vjp(energy_density, rho, sigma)
    vrho, vsigma = pull(jnp.ones_like(energy))
    along = jnp.sum(slope[:, :, None] * grads, axis=0)
    zeta = wts[:, None] * (0.5 * vrho[:, None] * values + 2.0 * vsigma[:, None] * along)
    return lax.dot_general(
        values,
        zeta,
        (((0,), (0,)), ((), ())),
        precision=highest,
        preferred_element_type=jnp.float32,
    )


def shards(basis_values, basis_grads, weights, tile_lists, tile_counts, owned_rows, density_slabs):
    devices = lax.axis_size("row")
    mine = lax.axis_index("row")
    tile = density_slabs.shape[0]
    slots = tile_lists.shape[1]
    ntiles = owned_rows.shape[0]
    funcs = slots * tile
    inverse = (
        jnp.zeros((ntiles,), jnp.int32).at[owned_rows].set(jnp.arange(ntiles, dtype=jnp.int32))
    )
    my_row = owned_rows[mine]
    used = jnp.arange(slots, dtype=jnp.int32)[None, :] < tile_counts[:, None]
    holds = jnp.any((tile_lists == my_row) & used, axis=1)
    keep = (holds[:, None] & used).astype(jnp.float32)
    tiles = density_slabs.reshape(tile, ntiles, tile)
    picked = jnp.take(tiles, tile_lists.reshape(-1), axis=1).reshape(tile, devices, slots, tile)
    outgoing = jnp.transpose(picked, (1, 0, 2, 3)) * keep[:, None, :, None]
    outgoing = outgoing.reshape(devices, tile, funcs)
    arrived = lax.all_to_all(outgoing, "row", split_axis=0, concat_axis=0, tiled=True)
    listed = tile_lists[mine]
    listed_used = used[mine]
    used_float = listed_used.astype(jnp.float32)
    block = jnp.take(arrived, inverse[listed], axis=0) * used_float[:, None, None]
    dens = block.reshape(funcs, funcs)
    piece = pbe_block(basis_values, basis_grads, weights, dens)
    mask = jnp.repeat(used_float, tile)
    piece = piece * mask[:, None] * mask[None, :]
    matches = (listed[None, :] == owned_rows[:, None]) & listed_used[None, :]
    present = jnp.any(matches, axis=1).astype(jnp.float32)
    position = jnp.argmax(matches, axis=1)
    rows_out = (
        jnp.take(piece.reshape(slots, tile, funcs), position, axis=0) * present[:, None, None]
    )
    returned = lax.all_to_all(rows_out, "row", split_axis=0, concat_axis=0, tiled=True)
    onehot = (tile_lists[:, :, None] == jnp.arange(ntiles, dtype=jnp.int32)[None, None, :]).astype(
        jnp.float32
    )
    summed = jnp.einsum(
        "sjc,stju->tcu",
        onehot,
        returned.reshape(devices, tile, slots, tile),
        precision=lax.Precision.HIGHEST,
    )
    column = jnp.transpose(jnp.take(summed, owned_rows, axis=1), (1, 0, 2))
    crossed = lax.all_to_all(column, "row", split_axis=0, concat_axis=0, tiled=True)
    mirrored = jnp.transpose(jnp.take(crossed, inverse, axis=0), (2, 0, 1))
    summed = summed + mirrored
    return summed.reshape(tile, ntiles * tile)


def solution(mesh):
    in_specs = (
        P(("parts", "row"), None),
        P(None, ("parts", "row"), None),
        P(("parts", "row")),
        P("parts", None),
        P("parts"),
        P("parts"),
        P(("parts", "row"), None),
    )
    out_specs = P(("parts", "row"), None)
    return jax.shard_map(shards, mesh=mesh, in_specs=in_specs, out_specs=out_specs, check_vma=False)
```

profile of v0, /device:TPU:0, one launch (start us, length us, event | category | flops | bytes accessed | tf_op | source)
XLA Modules:
  0.0 183.0 jit_solution(13554409790263557930)
XLA Ops:
  0.0 0.8 copy.53
  0.8 1.2 dynamic_slice.11
  2.0 1.4 compare_and_fusion
  3.3 0.7 and_convert_fusion
  4.3 1.1 reshape.215
  5.6 2.7 %gather_fusion.1 = f32[128,64,64]{2,1,0:T(8,128)} fusion(f32[64,16,64]{2,0,1:T(8,128)S(1)} %copy.54, s32[1024]{0:T(1024)S(1)} %pad_clamp_fusion.4), kind=kCustom, calls=%fused_computation.1 | custom fusion | bytes 4194816 | tf_op jit(solution)/shard_map/jit(_take)/gather | solution.py:54
  8.3 2.6 %multiply_bitcast_fusion = f32[16,64,8,64]{3,1,2,0:T(8,128)S(1)} fusion(f32[64,16,8,64]{3,0,2,1:T(8,128)} %bitcast.42, f32[16,8]{1,0:T(8,128)S(1)} %copy.55, pred[16,8]{1,0:T(8,128)(4,1)S(1)} %copy.52), kind=kLoop, calls=%fused_computation.9 | loop fusion | flops 1048576 | bytes 4194944 | tf_op jit(solution)/shard_map/mul | solution.py:55
  10.9 5.2 %copy.56 = f32[16,64,8,64]{3,2,1,0:T(8,128)} copy(f32[16,64,8,64]{3,1,2,0:T(8,128)S(1)} %multiply_bitcast_fusion) | data formatting | bytes 4194304 | tf_op jit(solution)/shard_map/mul | solution.py:55
  16.1 4.8 %reshape.217 = f32[16,64,512]{2,1,0:T(8,128)} reshape(f32[16,64,8,64]{3,2,1,0:T(8,128)} %copy.56) | data formatting | bytes 4194304 | tf_op jit(solution)/shard_map/reshape | solution.py:56
  20.9 7.6 %all-to-all-start = ((f32[16,64,512]{2,1,0:T(8,128)}), f32[16,64,512]{2,1,0:T(8,128)}, u32[]{:S(2)}, u32[]{:S(2)}) async-start(f32[16,64,512]{2,1,0:T(8,128)} %reshape.217), calls=%async_computation | async-start | bytes 4194304 | tf_op jit(solution)/shard_map/all_to_all | solution.py:57
  29.5 0.8 scatter_custom_fusion
  30.4 0.6 gather_fusion
  31.3 1.9 %copy.59 = f32[1024,512]{0,1:T(8,128)} copy(f32[1024,512]{1,0:T(8,128)S(1)} %copy-done) | data formatting | bytes 4194304 | tf_op args[0]
  33.3 36.3 %all-to-all-done = f32[16,64,512]{2,1,0:T(8,128)} async-done(((f32[16,64,512]{2,1,0:T(8,128)}), f32[16,64,512]{2,1,0:T(8,128)}, u32[]{:S(2)}, u32[]{:S(2)}) %all-to-all-start) | async-done | bytes 2097184 | tf_op jit(solution)/shard_map/all_to_all | solution.py:57
  69.7 2.2 %gather_fusion.2 = f32[8,64,512]{2,1,0:T(8,128)S(1)} fusion(f32[16,64,512]{2,1,0:T(8,128)} %all-to-all-done, s32[1024]{0:T(1024)S(1)} %pad_clamp_fusion.3), kind=kCustom, calls=%fused_computation.2 | custom fusion | bytes 2097184 | tf_op jit(solution)/shard_map/jit(_take)/gather | solution.py:61
  71.9 1.3 copy.57
  73.2 6.4 %multiply_reduce_fusion.2 = (f32[1024]{0:T(1024)S(1)}, f32[1024,512]{0,1:T(8,128)}) fusion(f32[1024,512]{0,1:T(8,128)} %copy.59, f32[1024,512]{1,0:T(8,128)S(1)} %copy-done, f32[512,512]{0,1:T(8,128)} %copy.57, f32[512]{0:T(512)S(1)} %mul.259, pred[512]{0:T(512)(128)(4,1)S(1)} %broadcast_in_dim.80), kind=kOutput, calls=%fused_computation.16 | convolution fusion | flops 3222797312 | bytes 7346688 | tf_op jit(solution)/shard_map/dot_general | solution.py:22
  79.6 2.9 %copy.58 = f32[1024,512]{1,0:T(8,128)} copy(f32[1024,512]{0,1:T(8,128)} %get-tuple-element.15) | data formatting | bytes 4194304 | tf_op jit(solution)/shard_map/dot_general | solution.py:22
  82.5 4.0 %multiply_reduce_fusion.1 = f32[3,1024]{1,0:T(4,128)S(1)} fusion(f32[3,1024,512]{2,1,0:T(8,128)} %param.8, f32[1024,512]{1,0:T(8,128)} %copy.58), kind=kLoop, calls=%fused_computation.8 | loop fusion | flops 3142656 | bytes 8400896 | tf_op jit(solution)/shard_map/reduce_sum | solution.py:24
  86.5 3.3 %multiply_reduce_fusion = f32[1024,512]{1,0:T(8,128)S(1)} fusion(f32[3,1024,512]{2,1,0:T(8,128)} %param.8, f32[3,1024]{1,0:T(4,128)S(1)} %get-tuple-element.8), kind=kLoop, calls=%fused_computation.7 | loop fusion | flops 2621440 | bytes 8400896 | tf_op jit(solution)/shard_map/reduce_sum | solution.py:28
  89.9 4.5 %fusion.8 = f32[512,512]{0,1:T(8,128)S(1)} fusion(f32[1024,512]{1,0:T(8,128)S(1)} %copy-done, f32[1024,512]{1,0:T(8,128)S(1)} %multiply_reduce_fusion, f32[1024]{0:T(1024)S(1)} %get-tuple-element.10, f32[1024]{0:T(1024)S(1)} %get-tuple-element.9, f32[1024]{0:T(1024)S(1)} %copy-done.3, f32[512]{0:T(512)S(1)} %mul.259), kind=kOutput, calls=%fused_computation.19 | convolution fusion | flops 3223846912 | bytes 5257216 | tf_op jit(solution)/shard_map/dot_general | solution.py:30
  94.5 0.7 gather_fusion.3
  95.2 1.7 select_multiply_fusion
  96.9 11.2 %all-to-all-start.1 = ((f32[16,64,512]{2,1,0:T(8,128)}), f32[16,64,512]{2,1,0:T(8,128)S(1)}, u32[]{:S(2)}, u32[]{:S(2)}) async-start(f32[16,64,512]{2,1,0:T(8,128)} %select_multiply_fusion), calls=%async_computation.1 | async-start | bytes 4194304 | tf_op jit(solution)/shard_map/all_to_all | solution.py:72
  108.1 41.1 %all-to-all-done.1 = f32[16,64,512]{2,1,0:T(8,128)S(1)} async-done(((f32[16,64,512]{2,1,0:T(8,128)}), f32[16,64,512]{2,1,0:T(8,128)S(1)}, u32[]{:S(2)}, u32[]{:S(2)}) %all-to-all-start.1) | async-done | bytes 2097184 | tf_op jit(solution)/shard_map/all_to_all | solution.py:72
  149.2 2.3 %reshape.219 = f32[16,64,8,64]{3,2,1,0:T(8,128)} reshape(f32[16,64,512]{2,1,0:T(8,128)S(1)} %all-to-all-done.1) | data formatting | bytes 4194304 | tf_op jit(solution)/shard_map/reshape | solution.py:79
  151.6 3.7 %convolution_bitcast_fusion.1 = f32[64,16,64]{2,1,0:T(8,128)S(1)} fusion(f32[16,64,8,64]{3,2,1,0:T(8,128)} %reshape.219, s32[16,8]{1,0:T(8,128)S(1)} %copy.53), kind=kOutput, calls=%fused_computation.20 | convolution fusion | flops 100665344 | bytes 2359808 | tf_op jit(solution)/shard_map/sjc,stju->tcu/dot_general | solution.py:76
  156.6 1.0 reshape.288
  157.6 11.2 %all-to-all-start.2 = ((f32[16,1,4096]{2,1,0:T(1,128)}), f32[16,1,4096]{2,1,0:T(1,128)S(1)}, u32[]{:S(2)}, u32[]{:S(2)}) async-start(f32[16,1,4096]{2,1,0:T(1,128)} %reshape.288), calls=%async_computation.2 | async-start | bytes 524288 | tf_op jit(solution)/shard_map/all_to_all | solution.py:83
  168.9 10.0 %all-to-all-done.2 = f32[16,1,4096]{2,1,0:T(1,128)S(1)} async-done(((f32[16,1,4096]{2,1,0:T(1,128)}), f32[16,1,4096]{2,1,0:T(1,128)S(1)}, u32[]{:S(2)}, u32[]{:S(2)}) %all-to-all-start.2) | async-done | bytes 262176 | tf_op jit(solution)/shard_map/all_to_all | solution.py:83
  179.4 1.3 reduce.24
  182.1 0.9 reshape.220
  (51 shorter events, 5.2 us)
Async XLA Ops:
  20.9 7.6 %copy-start.1 = (s32[16,8]{0,1:T(8,128)S(1)}, s32[16,8]{0,1:T(8,128)}, u32[]{:S(2)}) copy-start(s32[16,8]{0,1:T(8,128)} %param.10) | copy-start | bytes 1540
  20.9 8.0 %copy-start.2 = (s32[16]{0:T(128)S(1)}, s32[16]{0:T(128)}, u32[]{:S(2)}) copy-start(s32[16]{0:T(128)} %param.12) | copy-start | bytes 196
  20.9 10.4 %copy-start = (f32[1024,512]{1,0:T(8,128)S(1)}, f32[1024,512]{1,0:T(8,128)}, u32[]{:S(2)}) copy-start(f32[1024,512]{1,0:T(8,128)} %param.7) | copy-start | bytes 6291460
  20.9 48.7 %all-to-all-start = ((f32[16,64,512]{2,1,0:T(8,128)}), f32[16,64,512]{2,1,0:T(8,128)}, u32[]{:S(2)}, u32[]{:S(2)}) async-start(f32[16,64,512]{2,1,0:T(8,128)} %reshape.217), calls=%async_computation | async-start | bytes 4194304 | tf_op jit(solution)/shard_map/all_to_all | solution.py:57
  86.5 3.4 %copy-start.3 = (f32[1024]{0:T(1024)S(1)}, f32[1024]{0:T(1024)}, u32[]{:S(2)}) copy-start(f32[1024]{0:T(1024)} %param.9) | copy-start | bytes 12292
  96.9 52.3 %all-to-all-start.1 = ((f32[16,64,512]{2,1,0:T(8,128)}), f32[16,64,512]{2,1,0:T(8,128)S(1)}, u32[]{:S(2)}, u32[]{:S(2)}) async-start(f32[16,64,512]{2,1,0:T(8,128)} %select_multiply_fusion), calls=%async_computation.1 | async-start | bytes 4194304 | tf_op jit(solution)/shard_map/all_to_all | solution.py:72
  157.6 21.3 %all-to-all-start.2 = ((f32[16,1,4096]{2,1,0:T(1,128)}), f32[16,1,4096]{2,1,0:T(1,128)S(1)}, u32[]{:S(2)}, u32[]{:S(2)}) async-start(f32[16,1,4096]{2,1,0:T(1,128)} %reshape.288), calls=%async_computation.2 | async-start | bytes 524288 | tf_op jit(solution)/shard_map/all_to_all | solution.py:83
where the time goes:
time: 184 us; the launch traced here: 183 us
  waiting for transfers between devices  87.4 us (48%)
  local copies, waits for them, and re-layouts  34.6 us (19%)
  starting transfers between devices  30 us (16%)
  other arithmetic  16.1 us (9%)
  matrix products  14.6 us (8%)
    all_to_all x1, waiting for transfers between devices, shards(): lax.all_to_all(rows_out, 'row', split_axis=0, concat_axis=0, tiled=True)  41.1 us
    all_to_all x1, waiting for transfers between devices, shards(): lax.all_to_all(outgoing, 'row', split_axis=0, concat_axis=0, tiled=True)  36.3 us
    all_to_all x1, starting transfers between devices, shards(): lax.all_to_all(rows_out, 'row', split_axis=0, concat_axis=0, tiled=True)  11.2 us
    all_to_all x1, starting transfers between devices, shards(): lax.all_to_all(column, 'row', split_axis=0, concat_axis=0, tiled=True)  11.2 us
    all_to_all x1, waiting for transfers between devices, shards(): lax.all_to_all(column, 'row', split_axis=0, concat_axis=0, tiled=True)  10 us
    all_to_all x1, starting transfers between devices, shards(): lax.all_to_all(outgoing, 'row', split_axis=0, concat_axis=0, tiled=True)  7.58 us
    dot_general x1, matrix products, pbe_block(): jnp.dot(values, dens, precision=highest, preferred_element_type=jnp.float32)  6.36 us
    mul x1, local copies, waits for them, and re-layouts, shards(): outgoing = jnp.transpose(picked, (1, 0, 2, 3)) * keep[:, None, :, None]  5.2 us
  transfers between devices with their start and end apart: 3, of which 3 were waited for; matrix products, arithmetic and copies ran while one was open for 3% of the time, Pallas kernels for 0%

commit v1 on v0

v1 whole, which is shorter than its diff:
```python
import functools
import math

import jax
import jax.numpy as jnp
from jax import lax
from jax.experimental import pallas as pl
from jax.experimental.pallas import tpu as pltpu
from jax.sharding import PartitionSpec as P

KAPPA = 0.804
MU_COEF = 0.2195
COEF = 0.75 * (3.0 / math.pi) ** (1.0 / 3.0)
SCALE = 4.0 * (3.0 * math.pi**2) ** (2.0 / 3.0)
MESH = pl.DeviceIdType.MESH
VMEM_LIMIT = 60 * 1024 * 1024
F32, BF16 = jnp.float32, jnp.bfloat16


def pair(load, first, second, tile):
    left, right = load(lax.div(first, 2)), load(lax.div(second, 2))
    low = lax.broadcasted_iota(jnp.int32, left.shape, 1) < tile
    odd = jnp.full(left.shape, lax.rem(first, 2), jnp.int32) == 1
    even = jnp.full(left.shape, lax.rem(second, 2), jnp.int32) == 0
    left = jnp.where(odd, pltpu.roll(left, tile, 1), left)
    right = jnp.where(even, pltpu.roll(right, tile, 1), right)
    return jnp.where(low, left, right)


def place(n):
    me = lax.axis_index("row")
    return me, me // 4, (me // 2) % 2, me % 2


def to(row):
    return {"row": row}


def greet(planes, me, z, y, c):
    barrier = pltpu.get_barrier_semaphore()
    for ok, peer in neighbours(planes, me, z, y, c):
        @pl.when(ok)
        def _():
            pl.semaphore_signal(barrier, inc=1, device_id=to(peer), device_id_type=MESH)
    peers = 2 + (z > 0).astype(jnp.int32) + (z < planes - 1).astype(jnp.int32)
    pl.semaphore_wait(barrier, peers)


def neighbours(planes, me, z, y, c):
    return (
        (z >= 0, me + 1 - 2 * c),
        (z >= 0, me + 2 - 4 * y),
        (z > 0, me - 4),
        (z < planes - 1, me + 4),
    )


def pack_kernel(n, slab_ref, owned_ref, own_ref):
    groups, tile, lanes = own_ref.shape
    me = lax.axis_index("row")
    for g in range(groups):
        chip = lax.rem(me // 2 + g, n // 2)
        own_ref[g] = pair(
            lambda q: slab_ref[:, pl.ds(pl.multiple_of(q * lanes, lanes), lanes)],
            owned_ref[2 * chip],
            owned_ref[2 * chip + 1],
            tile,
        )


def order_kernel(line_ref, inv_ref, out_ref):
    chips, tile, lanes = line_ref.shape
    for q in range(chips):
        out_ref[:, q * lanes : (q + 1) * lanes] = pair(
            lambda p: line_ref[p], inv_ref[2 * q], inv_ref[2 * q + 1], tile
        )


def gather_kernel(n, own_ref, full_ref, buf, send_sem, recv_sem):
    planes, chips = n // 4, n // 2
    groups = buf.shape[1]
    lanes = buf.shape[3]
    me, z, y, c = place(n)
    core_peer, side_peer = me + 1 - 2 * c, me + 2 - 4 * y
    buf[me] = own_ref[...]
    greet(planes, me, z, y, c)

    def copy(s, way, peer):
        return pltpu.make_async_remote_copy(
            src_ref=buf.at[s],
            dst_ref=buf.at[s],
            send_sem=send_sem.at[way, s],
            recv_sem=recv_sem.at[s],
            device_id=to(peer),
            device_id_type=MESH,
        )

    def arrive(s):
        copy(s, 0, core_peer).wait_recv()

    up, down = z < planes - 1, z > 0

    def along(k, fn):
        for sign in (1, -1):
            zz = z + sign * k
            @pl.when((zz >= 0) & (zz < planes))
            def _():
                fn(zz, sign)
            if k == 0:
                break

    @pl.when(up)
    def _():
        copy(me, 3, me + 4).start()

    @pl.when(down)
    def _():
        copy(me, 2, me - 4).start()

    copy(me, 1, side_peer).start()
    copy(me, 0, core_peer).start()

    def from_side(zz, sign):
        s = (zz * 2 + 1 - y) * 2 + c
        arrive(s)
        copy(s, 0, core_peer).start()

    for k in range(1, planes):
        def from_plane(zz, sign):
            s = (zz * 2 + y) * 2 + c
            arrive(s)
            if k < planes - 1:
                if sign > 0:
                    @pl.when(down)
                    def _():
                        copy(s, 2, me - 4).start()
                else:
                    @pl.when(up)
                    def _():
                        copy(s, 3, me + 4).start()
            copy(s, 1, side_peer).start()
            copy(s, 0, core_peer).start()

        along(k, from_plane)
        along(k - 1, from_side)
    along(planes - 1, from_side)
    for k in range(planes):
        def from_core(zz, sign):
            for side in range(2):
                arrive((zz * 2 + side) * 2 + 1 - c)

        along(k, from_core)

    @pl.loop(0, chips)
    def _(m):
        rows = pl.ds(pl.multiple_of(m * lanes, lanes), lanes)
        for g in range(groups):
            other = lax.rem(m + g, chips)
            cols = pl.ds(pl.multiple_of(other * lanes, lanes), lanes)
            block = jnp.concatenate([buf[2 * m, g], buf[2 * m + 1, g]], axis=0)
            full_ref[rows, cols] = block
            if g and 2 * g != chips:
                full_ref[cols, rows] = block.T

    for k in range(planes):
        def sent(zz, sign):
            s = (zz * 2 + y) * 2 + c
            copy(s, 0, core_peer).wait_send()
            copy(s, 1, side_peer).wait_send()
            copy((zz * 2 + 1 - y) * 2 + c, 0, core_peer).wait_send()
            if k == 0 or (k < planes - 1 and sign < 0):
                @pl.when(up)
                def _():
                    copy(s, 3, me + 4).wait_send()
            if k == 0 or (k < planes - 1 and sign > 0):
                @pl.when(down)
                def _():
                    copy(s, 2, me - 4).wait_send()

        along(k, sent)


def compute_kernel(
    n, groups, full_ref, lists_ref, counts_ref, owned_ref, phi_ref, grad_ref, wts_ref,
    out_ref, inv_out, high, lows, acc, inv, pos, has,
):
    step = pl.program_id(0)
    slots = lists_ref.shape[1]
    funcs = phi_ref.shape[1]
    tile = funcs // slots
    lanes = 2 * tile
    chips = n // 2
    me = lax.axis_index("row")

    @pl.when(step == 0)
    def _():
        count = counts_ref[me]

        @pl.loop(0, n)
        def _(r):
            inv[owned_ref[r]] = r
            pos[r] = 0
            has[r] = 0

        @pl.loop(0, n)
        def _(r):
            inv_out[r] = inv[r]

        for k in range(slots):
            owner = inv[lists_ref[me, k]]
            pos[owner] = k
            has[owner] = (k < count).astype(jnp.int32)

        @pl.loop(0, slots)
        def _(i):
            rows = pl.ds(pl.multiple_of(inv[lists_ref[me, i]] * tile, tile), tile)
            dest = pl.ds(pl.multiple_of(i * tile, tile), tile)
            for j in range(slots // 2):
                block = pair(
                    lambda q: full_ref[rows, pl.ds(pl.multiple_of(q * lanes, lanes), lanes)],
                    inv[lists_ref[me, 2 * j]],
                    inv[lists_ref[me, 2 * j + 1]],
                    tile,
                )
                slot = 2 * j + lax.broadcasted_iota(jnp.int32, block.shape, 1) // tile
                keep = (slot < count) & (jnp.full(block.shape, i, jnp.int32) < count)
                block = jnp.where(keep, block, 0.0)
                top = block.astype(BF16)
                high[dest, j * lanes : (j + 1) * lanes] = top
                lows[dest, j * lanes : (j + 1) * lanes] = (block - top.astype(F32)).astype(BF16)

        acc[...] = jnp.zeros_like(acc)

    phi = phi_ref[...]
    phi_high = phi.astype(BF16)
    phi_low = (phi - phi_high.astype(F32)).astype(BF16)

    def dot(a, b):
        return jnp.dot(a, b, preferred_element_type=F32)

    mixed = dot(phi_high, high[...]) + dot(phi_high, lows[...]) + dot(phi_low, high[...])

    def row_sum(prod):
        part = prod[:, :lanes]
        for q in range(1, funcs // lanes):
            part = part + prod[:, q * lanes : (q + 1) * lanes]
        return jnp.sum(part.T, axis=0, keepdims=True)

    rho = row_sum(mixed * phi)
    slope = [2.0 * row_sum(mixed * grad_ref[k]) for k in range(3)]
    sigma = slope[0] * slope[0] + slope[1] * slope[1] + slope[2] * slope[2]
    root = jnp.exp(jnp.log(rho) * (1.0 / 3.0))
    four = rho * root
    reduced = sigma / (SCALE * (four * four))
    inner = 1.0 / (1.0 + (MU_COEF / KAPPA) * reduced)
    factor = 1.0 + KAPPA - KAPPA * inner
    change = MU_COEF * inner
    vrho = -COEF * root * ((4.0 / 3.0) * factor - (8.0 / 3.0) * ((reduced * inner) * change))
    vsigma = (-COEF / SCALE) * (change * inner) / four
    wts = wts_ref[...]
    rows = [0.5 * wts * vrho] + [2.0 * wts * vsigma * s for s in slope]
    scal = jnp.concatenate(rows + rows, axis=0).T
    zeta = (
        scal[:, 0:1] * phi
        + scal[:, 1:2] * grad_ref[0]
        + scal[:, 2:3] * grad_ref[1]
        + scal[:, 3:4] * grad_ref[2]
    )
    zeta_high = zeta.astype(BF16)
    zeta_low = (zeta - zeta_high.astype(F32)).astype(BF16)

    def tdot(a, b):
        return lax.dot_general(a, b, (((0,), (0,)), ((), ())), preferred_element_type=F32)

    acc[...] += tdot(phi_high, zeta_high) + tdot(phi_high, zeta_low) + tdot(phi_low, zeta_high)

    @pl.when(step == pl.num_programs(0) - 1)
    def _():
        acc[...] = acc[...] + acc[...].T

        @pl.loop(0, n)
        def _(r):
            rows = pl.ds(pl.multiple_of(pos[r] * tile, tile), tile)
            for g in range(groups):
                chip = lax.rem(r // 2 + g, chips)
                block = pair(
                    lambda q: acc[rows, pl.ds(pl.multiple_of(q * lanes, lanes), lanes)],
                    pos[2 * chip],
                    pos[2 * chip + 1],
                    tile,
                )
                low = lax.broadcasted_iota(jnp.int32, block.shape, 1) < tile
                keep = jnp.where(
                    low,
                    jnp.full(block.shape, has[r] * has[2 * chip], jnp.int32),
                    jnp.full(block.shape, has[r] * has[2 * chip + 1], jnp.int32),
                )
                out_ref[r, g] = jnp.where(keep == 1, block, 0.0)


def reduce_kernel(
    n, part_ref, line, core_in, side_in, plane_in, msg, got,
    core_sem, side_sem, plane_sem, msg_sem,
):
    planes, chips = n // 4, n // 2
    groups, tile = part_ref.shape[1], part_ref.shape[2]
    lanes = 2 * tile
    half = tile // 2
    me, z, y, c = place(n)
    core_peer, side_peer = me + 1 - 2 * c, me + 2 - 4 * y
    chip = me // 2
    mirrored = [g for g in range(1, groups) if 2 * g != chips]

    barrier = pltpu.get_barrier_semaphore()

    @pl.loop(1, n)
    def _(k):
        pl.semaphore_signal(
            barrier, inc=1, device_id=to(lax.rem(me + k, n)), device_id_type=MESH
        )

    pl.semaphore_wait(barrier, n - 1)

    def remote(src, dst, sems, slot, peer):
        return pltpu.make_async_remote_copy(
            src_ref=src, dst_ref=dst, send_sem=sems.at[0, slot], recv_sem=sems.at[1, slot],
            device_id=to(peer), device_id_type=MESH,
        )

    def by_core(zz, side):
        j = zz * 2 + side
        return remote(part_ref.at[2 * j + 1 - c], core_in.at[j], core_sem, j, core_peer)

    def by_side(zz):
        return remote(core_in.at[zz * 2 + 1 - y], side_in.at[zz], side_sem, zz, side_peer)

    def by_plane(zz, sign):
        way = 0 if sign > 0 else 1
        return remote(
            side_in.at[zz], plane_in.at[way, zz], plane_sem, way * planes + zz, me + 4 * sign
        )

    def far_to_near(fn):
        for k in range(planes - 1, -1, -1):
            for sign in (1, -1):
                zz = z + sign * k
                @pl.when((zz >= 0) & (zz < planes))
                def _():
                    fn(zz, k, sign)
                if k == 0:
                    break

    def start_core(zz, k, sign):
        by_core(zz, 1 - y).start()
        by_core(zz, y).start()

    far_to_near(start_core)

    def side_step(zz, k, sign):
        by_core(zz, 1 - y).wait_recv()
        j = zz * 2 + 1 - y
        core_in[j] = core_in[j] + part_ref[2 * j + c]
        by_side(zz).start()

    far_to_near(side_step)

    def plane_step(zz, k, sign):
        by_core(zz, y).wait_recv()
        j = zz * 2 + y
        core_in[j] = core_in[j] + part_ref[2 * j + c]
        by_side(zz).wait_recv()
        side_in[zz] = side_in[zz] + core_in[j]
        if k:
            behind = (z > 0) if sign > 0 else (z < planes - 1)

            @pl.when(behind)
            def _():
                by_plane(zz, sign).wait_recv()
                side_in[zz] = side_in[zz] + plane_in[0 if sign > 0 else 1, zz]

            by_plane(zz, sign).start()

    far_to_near(plane_step)

    for ok, sign in ((z > 0, 1), (z < planes - 1, -1)):
        @pl.when(ok)
        def _():
            by_plane(z, sign).wait_recv()
            side_in[z] = side_in[z] + plane_in[0 if sign > 0 else 1, z]

    def by_mirror(i, g, core):
        return pltpu.make_async_remote_copy(
            src_ref=msg.at[i, core],
            dst_ref=got.at[i, c],
            send_sem=msg_sem.at[0, 2 * i + core],
            recv_sem=msg_sem.at[1, 2 * i + c],
            device_id=to(lax.rem(chip + g, chips) * 2 + core),
            device_id_type=MESH,
        )

    for i, g in enumerate(mirrored):
        for core in range(2):
            block = side_in[z, g, :, core * tile : (core + 1) * tile]
            msg[i, core] = jnp.concatenate([block[:half], block[half:]], axis=1)
            by_mirror(i, g, core).start()
    for g in range(groups):
        line[lax.rem(chip + g, chips)] = side_in[z, g]
    for i, g in enumerate(mirrored):
        blocks = []
        for core in range(2):
            pltpu.make_async_remote_copy(
                src_ref=msg.at[i, core],
                dst_ref=got.at[i, core],
                send_sem=msg_sem.at[0, 2 * i + core],
                recv_sem=msg_sem.at[1, 2 * i + core],
                device_id=to(core_peer),
                device_id_type=MESH,
            ).wait_recv()
            wide = got[i, core]
            blocks.append(jnp.concatenate([wide[:, :tile], wide[:, tile:]], axis=0))
        line[lax.rem(chip + chips - g, chips)] = jnp.concatenate(blocks, axis=0).T
    def sent(zz, k, sign):
        by_core(zz, y).wait_send()
        by_core(zz, 1 - y).wait_send()
        by_side(zz).wait_send()
        if k:
            by_plane(zz, sign).wait_send()

    far_to_near(sent)
    for i, g in enumerate(mirrored):
        for core in range(2):
            by_mirror(i, g, core).wait_send()


def shards(basis_values, basis_grads, weights, tile_lists, tile_counts, owned_rows, density_slabs):
    n = lax.axis_size("row")
    tile, width = density_slabs.shape
    npts, funcs = basis_values.shape
    planes, chips = n // 4, n // 2
    groups = chips // 2 + 1
    lanes = 2 * tile
    vmem = pl.BlockSpec(memory_space=pltpu.VMEM)
    smem = pl.BlockSpec(memory_space=pltpu.SMEM)
    dma = pltpu.SemaphoreType.DMA
    own = pl.pallas_call(
        functools.partial(pack_kernel, n),
        out_shape=jax.ShapeDtypeStruct((groups, tile, lanes), F32),
        in_specs=[vmem, smem],
        out_specs=vmem,
        name="pack_density",
    )(density_slabs, owned_rows)
    full = pl.pallas_call(
        functools.partial(gather_kernel, n),
        out_shape=jax.ShapeDtypeStruct((width, width), F32),
        in_specs=[vmem],
        out_specs=vmem,
        scratch_shapes=[
            pltpu.VMEM((n, groups, tile, lanes), F32),
            dma((4, n)),
            dma((n,)),
        ],
        compiler_params=pltpu.CompilerParams(
            collective_id=0, has_side_effects=True, vmem_limit_bytes=VMEM_LIMIT
        ),
        name="gather_density",
    )(own)
    chunk = min(npts, 256)
    part, inv = pl.pallas_call(
        functools.partial(compute_kernel, n, groups),
        grid=(npts // chunk,),
        out_shape=(
            jax.ShapeDtypeStruct((n, groups, tile, lanes), F32),
            jax.ShapeDtypeStruct((n,), jnp.int32),
        ),
        in_specs=[
            vmem, smem, smem, smem,
            pl.BlockSpec((chunk, funcs), lambda i: (i, 0)),
            pl.BlockSpec((3, chunk, funcs), lambda i: (0, i, 0)),
            pl.BlockSpec((1, chunk), lambda i: (0, i)),
        ],
        out_specs=(vmem, smem),
        scratch_shapes=[
            pltpu.VMEM((funcs, funcs), BF16),
            pltpu.VMEM((funcs, funcs), BF16),
            pltpu.VMEM((funcs, funcs), F32),
            pltpu.SMEM((n,), jnp.int32),
            pltpu.SMEM((n,), jnp.int32),
            pltpu.SMEM((n,), jnp.int32),
        ],
        compiler_params=pltpu.CompilerParams(vmem_limit_bytes=VMEM_LIMIT),
        name="batch_potential",
    )(
        full, tile_lists, tile_counts, owned_rows,
        basis_values, basis_grads, weights.reshape(1, npts),
    )
    mirrored = len([g for g in range(1, groups) if 2 * g != chips])
    line = pl.pallas_call(
        functools.partial(reduce_kernel, n),
        out_shape=jax.ShapeDtypeStruct((chips, tile, lanes), F32),
        in_specs=[vmem],
        out_specs=vmem,
        scratch_shapes=[
            pltpu.VMEM((chips, groups, tile, lanes), F32),
            pltpu.VMEM((planes, groups, tile, lanes), F32),
            pltpu.VMEM((2, planes, groups, tile, lanes), F32),
            pltpu.VMEM((mirrored, 2, tile // 2, lanes), F32),
            pltpu.VMEM((mirrored, 2, tile // 2, lanes), F32),
            dma((2, chips)),
            dma((2, planes)),
            dma((2, 2 * planes)),
            dma((2, 2 * mirrored)),
        ],
        compiler_params=pltpu.CompilerParams(
            collective_id=1, has_side_effects=True, vmem_limit_bytes=VMEM_LIMIT
        ),
        name="reduce_potential",
    )(part)
    return pl.pallas_call(
        order_kernel,
        out_shape=jax.ShapeDtypeStruct((tile, width), F32),
        in_specs=[vmem, smem],
        out_specs=vmem,
        name="order_columns",
    )(line, inv)


def solution(mesh):
    in_specs = (
        P(("parts", "row"), None),
        P(None, ("parts", "row"), None),
        P(("parts", "row")),
        P("parts", None),
        P("parts"),
        P("parts"),
        P(("parts", "row"), None),
    )
    out_specs = P(("parts", "row"), None)
    return jax.shard_map(shards, mesh=mesh, in_specs=in_specs, out_specs=out_specs, check_vma=False)
```

time: 184 us -> 80.8 us (0.44)
  waiting for transfers between devices: 87.4 us -> 0 us
  Pallas kernels: 0 us -> 79.2 us
  local copies, waits for them, and re-layouts: 34.6 us -> 1.35 us
  starting transfers between devices: 30 us -> 0 us
  other arithmetic: 16.1 us -> 0 us
  matrix products: 14.6 us -> 0 us
    all_to_all x3 -> x0, waiting for transfers between devices: 87.4 us -> none  [the longest x1 41.1 us: shards(): lax.all_to_all(rows_out, 'row', split_axis=0, concat_axis=0, tiled=True)]
    pallas_call x0 -> x5, Pallas kernels: none -> 79.2 us  [the longest x1 31.5 us: shards(): pl.pallas_call(functools.partial(reduce_kernel, n), out_shape=jax.ShapeDt...]
    all_to_all x3 -> x0, starting transfers between devices: 30 us -> none  [the longest x1 11.2 us: shards(): lax.all_to_all(rows_out, 'row', split_axis=0, concat_axis=0, tiled=True)]
    dot_general x3 -> x0, matrix products: 14.6 us -> none  [the longest x1 6.36 us: pbe_block(): jnp.dot(values, dens, precision=highest, preferred_element_type=jnp.float32)]
    reshape x6 -> x0, local copies, waits for them, and re-layouts: 9.36 us -> none  [the longest x1 4.79 us: shards(): outgoing = outgoing.reshape(devices, tile, funcs)]
    gather x9 -> x0, local copies, waits for them, and re-layouts: 9.29 us -> none  [the longest x2 3.52 us: shards(): jnp.take(arrived, inverse[listed], axis=0) * used_float[:, None, None]]
    reduce_sum x3 -> x0, other arithmetic: 7.39 us -> none  [the longest x1 4.04 us: pbe_block(): slope = 2.0 * jnp.sum(mixed[None, :, :] * grads, axis=2)]
    mul x3 -> x0, local copies, waits for them, and re-layouts: 5.35 us -> none  [the longest x1 5.2 us: shards(): outgoing = jnp.transpose(picked, (1, 0, 2, 3)) * keep[:, None, :, None]]
  transfers between devices with their start and end apart: 3 -> 0, of which waited for: 3 -> 0; matrix products, arithmetic and copies ran while one was open for 3% -> 0% of each run, Pallas kernels for 0% -> 0%
where the time goes in v1:
time: 80.8 us; the launch traced here: 80.5 us
  Pallas kernels  79.2 us (98%)
  local copies, waits for them, and re-layouts  1.35 us (2%)
    pallas_call x1, Pallas kernels, shards(): pl.pallas_call(functools.partial(reduce_kernel, n), out_shape=jax.ShapeDt...  31.5 us
    pallas_call x1, Pallas kernels, shards(): pl.pallas_call(functools.partial(gather_kernel, n), out_shape=jax.ShapeDt...  27.8 us
    pallas_call x1, Pallas kernels, shards(): pl.pallas_call(functools.partial(compute_kernel, n, groups), grid=(npts /...  16.2 us
    pallas_call x1, Pallas kernels, shards(): pl.pallas_call(order_kernel, out_shape=jax.ShapeDtypeStruct((tile, width)...  1.87 us
    pallas_call x1, Pallas kernels, shards(): pl.pallas_call(functools.partial(pack_kernel, n), out_shape=jax.ShapeDtyp...  1.8 us

profile of v1, /device:TPU:0, one launch (start us, length us, event | category | flops | bytes accessed | tf_op | source)
XLA Modules:
  0.0 80.5 jit_solution(4406736362309739510)
XLA Ops:
  0.0 1.4 %copy.8.lists_ref = s32[16,8]{1,0:T(8,128)} copy(s32[16,8]{0,1:T(8,128)} %param.10) | data formatting | bytes 1024 | tf_op args[3]
  1.4 1.8 %pack_density.1.own_ref = f32[5,64,128]{2,1,0:T(8,128)} custom-call(f32[64,1024]{1,0:T(8,128)} %slab_ref.1, s32[16]{0:T(128)} %owned_ref.3), custom_call_target="tpu_custom_call" | custom-call | tf_op jit(solution)/shard_map/pack_density/pallas_call | solution.py:445
  3.2 27.8 %gather_density.1.full_ref = f32[1024,1024]{1,0:T(8,128)} custom-call(f32[5,64,128]{2,1,0:T(8,128)} %pack_density.1.own_ref), custom_call_target="tpu_custom_call" | custom-call | tf_op jit(solution)/shard_map/gather_density/pallas_call | solution.py:452
  31.0 16.2 %batch_potential.1 = (f32[16,5,64,128]{3,2,1,0:T(8,128)}, s32[16]{0:T(128)}) custom-call(f32[1024,1024]{1,0:T(8,128)} %gather_density.1.full_ref, s32[16,8]{1,0:T(8,128)} %copy.8.lists_ref, s32[16]{0:T(128)} %counts_ref.1, s32[16]{0:T(128)} %owned_ref.3, f32[1024,512]{1,0:T(8,128)} %phi_ref.1, f32[3,1024,512]{2,1,0:T(8,128)} %grad_ref.1, f32[1,1024]{1,0:T(1,128)} %bitcast.1), custom_call_target="tpu_custom_call" | custom-call | tf_op jit(solution)/shard_map/batch_potential/pallas_call | solution.py:468
  47.2 31.5 %reduce_potential.1.line_ref = f32[8,64,128]{2,1,0:T(8,128)} custom-call(f32[16,5,64,128]{3,2,1,0:T(8,128)} %get-tuple-element.7.part_ref), custom_call_target="tpu_custom_call" | custom-call | tf_op jit(solution)/shard_map/reduce_potential/pallas_call | solution.py:497
  78.7 1.9 %order_columns.1 = f32[64,1024]{1,0:T(8,128)} custom-call(f32[8,64,128]{2,1,0:T(8,128)} %reduce_potential.1.line_ref, s32[16]{0:T(128)} %get-tuple-element.8.inv_ref), custom_call_target="tpu_custom_call" | custom-call | tf_op jit(solution)/shard_map/order_columns/pallas_call | solution.py:518

commit v2 on v1

--- a/solution.py
+++ b/solution.py
@@ -13,6 +13,7 @@
 COEF = 0.75 * (3.0 / math.pi) ** (1.0 / 3.0)
 SCALE = 4.0 * (3.0 * math.pi**2) ** (2.0 / 3.0)
 MESH = pl.DeviceIdType.MESH
+PIECES = 2
 VMEM_LIMIT = 60 * 1024 * 1024
 F32, BF16 = jnp.float32, jnp.bfloat16
 
@@ -27,6 +28,25 @@
     return jnp.where(low, left, right)
 
 
+def cut(groups):
+    return [groups * h // PIECES for h in range(PIECES + 1)]
+
+
+def chosen(columns, first, second, tile):
+    shape = columns[0].shape
+    low = lax.broadcasted_iota(jnp.int32, shape, 1) < tile
+    want = jnp.where(low, jnp.full(shape, first, jnp.int32), jnp.full(shape, second, jnp.int32))
+    straight = jnp.where(low, 0, 1)
+    same = jnp.zeros(shape, F32)
+    swap = jnp.zeros(shape, F32)
+    back = pltpu.roll(want, tile, 1)
+    for q, column in enumerate(columns):
+        same = jnp.where(want == 2 * q + straight, column, same)
+        swap = jnp.where(back == 2 * q + straight, column, swap)
+    turned = pltpu.roll(swap, tile, 1)
+    return jnp.where(want % 2 == straight, same, turned)
+
+
 def place(n):
     me = lax.axis_index("row")
     return me, me // 4, (me // 2) % 2, me % 2
@@ -55,48 +75,33 @@
     )
 
 
-def pack_kernel(n, slab_ref, owned_ref, own_ref):
-    groups, tile, lanes = own_ref.shape
-    me = lax.axis_index("row")
-    for g in range(groups):
-        chip = lax.rem(me // 2 + g, n // 2)
-        own_ref[g] = pair(
-            lambda q: slab_ref[:, pl.ds(pl.multiple_of(q * lanes, lanes), lanes)],
-            owned_ref[2 * chip],
-            owned_ref[2 * chip + 1],
-            tile,
-        )
-
-
-def order_kernel(line_ref, inv_ref, out_ref):
-    chips, tile, lanes = line_ref.shape
-    for q in range(chips):
-        out_ref[:, q * lanes : (q + 1) * lanes] = pair(
-            lambda p: line_ref[p], inv_ref[2 * q], inv_ref[2 * q + 1], tile
-        )
-
-
-def gather_kernel(n, own_ref, full_ref, buf, send_sem, recv_sem):
+def gather_kernel(n, slab_ref, owned_ref, full_ref, buf, send_sem, recv_sem):
     planes, chips = n // 4, n // 2
     groups = buf.shape[1]
     lanes = buf.shape[3]
+    cuts = cut(groups)
+    halves = range(len(cuts) - 1)
     me, z, y, c = place(n)
     core_peer, side_peer = me + 1 - 2 * c, me + 2 - 4 * y
-    buf[me] = own_ref[...]
+    columns = [slab_ref[:, q * lanes : (q + 1) * lanes] for q in range(chips)]
+    for g in range(groups):
+        chip = lax.rem(me // 2 + g, chips)
+        buf[me, g] = chosen(columns, owned_ref[2 * chip], owned_ref[2 * chip + 1], lanes // 2)
     greet(planes, me, z, y, c)
 
-    def copy(s, way, peer):
+    def copy(s, way, peer, h):
+        part = buf.at[s, pl.ds(cuts[h], cuts[h + 1] - cuts[h])]
         return pltpu.make_async_remote_copy(
-            src_ref=buf.at[s],
-            dst_ref=buf.at[s],
-            send_sem=send_sem.at[way, s],
-            recv_sem=recv_sem.at[s],
+            src_ref=part,
+            dst_ref=part,
+            send_sem=send_sem.at[h, way, s],
+            recv_sem=recv_sem.at[h, s],
             device_id=to(peer),
             device_id_type=MESH,
         )
 
-    def arrive(s):
-        copy(s, 0, core_peer).wait_recv()
+    def arrive(s, h):
+        copy(s, 0, core_peer, h).wait_recv()
 
     up, down = z < planes - 1, z > 0
 
@@ -109,45 +114,80 @@
             if k == 0:
                 break
 
-    @pl.when(up)
-    def _():
-        copy(me, 3, me + 4).start()
-
-    @pl.when(down)
-    def _():
-        copy(me, 2, me - 4).start()
-
-    copy(me, 1, side_peer).start()
-    copy(me, 0, core_peer).start()
-
-    def from_side(zz, sign):
+    for h in halves:
+        @pl.when(up)
+        def _():
+            copy(me, 3, me + 4, h).start()
+
+        @pl.when(down)
+        def _():
+            copy(me, 2, me - 4, h).start()
+
+        copy(me, 1, side_peer, h).start()
+        copy(me, 0, core_peer, h).start()
+
+    def ends(zz):
+        return (zz == 0) | (zz == planes - 1)
+
+    def crossed(zz, sign, k, h, act):
         s = (zz * 2 + 1 - y) * 2 + c
-        arrive(s)
-        copy(s, 0, core_peer).start()
-
-    for k in range(1, planes):
-        def from_plane(zz, sign):
+        if h == len(cuts) - 2:
+            if k == 0 or sign < 0:
+                @pl.when(ends(zz) & up)
+                def _():
+                    act(copy(s, 3, me + 4, h))
+            if k == 0 or sign > 0:
+                @pl.when(ends(zz) & down)
+                def _():
+                    act(copy(s, 2, me - 4, h))
+
+    def over(zz, k, h, act):
+        s = (zz * 2 + y) * 2 + c
+        if k and h == len(cuts) - 2:
+            @pl.when(jnp.logical_not(ends(zz)))
+            def _():
+                act(copy(s, 1, side_peer, h))
+        else:
+            act(copy(s, 1, side_peer, h))
+
+    def from_side(k, h):
+        def fn(zz, sign):
+            s = (zz * 2 + 1 - y) * 2 + c
+            arrive(s, h)
+            crossed(zz, sign, k, h, lambda copied: copied.start())
+            copy(s, 0, core_peer, h).start()
+
+        return fn
+
+    def from_plane(k, h):
+        def fn(zz, sign):
             s = (zz * 2 + y) * 2 + c
-            arrive(s)
+            arrive(s, h)
             if k < planes - 1:
                 if sign > 0:
                     @pl.when(down)
                     def _():
-                        copy(s, 2, me - 4).start()
+                        copy(s, 2, me - 4, h).start()
                 else:
                     @pl.when(up)
                     def _():
-                        copy(s, 3, me + 4).start()
-            copy(s, 1, side_peer).start()
-            copy(s, 0, core_peer).start()
-
-        along(k, from_plane)
-        along(k - 1, from_side)
-    along(planes - 1, from_side)
+                        copy(s, 3, me + 4, h).start()
+            over(zz, k, h, lambda copied: copied.start())
+            copy(s, 0, core_peer, h).start()
+
+        return fn
+
+    for k in range(1, planes):
+        for h in halves:
+            along(k, from_plane(k, h))
+            along(k - 1, from_side(k - 1, h))
+    for h in halves:
+        along(planes - 1, from_side(planes - 1, h))
     for k in range(planes):
         def from_core(zz, sign):
             for side in range(2):
-                arrive((zz * 2 + side) * 2 + 1 - c)
+                for h in halves:
+                    arrive((zz * 2 + side) * 2 + 1 - c, h)
 
         along(k, from_core)
 
@@ -163,29 +203,31 @@
                 full_ref[cols, rows] = block.T
 
     for k in range(planes):
-        def sent(zz, sign):
-            s = (zz * 2 + y) * 2 + c
-            copy(s, 0, core_peer).wait_send()
-            copy(s, 1, side_peer).wait_send()
-            copy((zz * 2 + 1 - y) * 2 + c, 0, core_peer).wait_send()
-            if k == 0 or (k < planes - 1 and sign < 0):
-                @pl.when(up)
-                def _():
-                    copy(s, 3, me + 4).wait_send()
-            if k == 0 or (k < planes - 1 and sign > 0):
-                @pl.when(down)
-                def _():
-                    copy(s, 2, me - 4).wait_send()
-
-        along(k, sent)
+        for h in halves:
+            def sent(zz, sign):
+                s = (zz * 2 + y) * 2 + c
+                copy(s, 0, core_peer, h).wait_send()
+                over(zz, k, h, lambda copied: copied.wait_send())
+                crossed(zz, sign, k, h, lambda copied: copied.wait_send())
+                copy((zz * 2 + 1 - y) * 2 + c, 0, core_peer, h).wait_send()
+                if k == 0 or (k < planes - 1 and sign < 0):
+                    @pl.when(up)
+                    def _():
+                        copy(s, 3, me + 4, h).wait_send()
+                if k == 0 or (k < planes - 1 and sign > 0):
+                    @pl.when(down)
+                    def _():
+                        copy(s, 2, me - 4, h).wait_send()
+
+            along(k, sent)
 
 
 def compute_kernel(
     n, groups, full_ref, lists_ref, counts_ref, owned_ref, phi_ref, grad_ref, wts_ref,
-    out_ref, inv_out, high, lows, acc, inv, pos, has,
+    out_ref, inv_out, high, lows, acc, turned, inv, pos, has,
 ):
     step = pl.program_id(0)
-    slots = lists_ref.shape[1]
+    slots = lists_ref.shape[0]
     funcs = phi_ref.shape[1]
     tile = funcs // slots
     lanes = 2 * tile
@@ -207,19 +249,19 @@
             inv_out[r] = inv[r]
 
         for k in range(slots):
-            owner = inv[lists_ref[me, k]]
+            owner = inv[lists_ref[k, me]]
             pos[owner] = k
             has[owner] = (k < count).astype(jnp.int32)
 
         @pl.loop(0, slots)
         def _(i):
-            rows = pl.ds(pl.multiple_of(inv[lists_ref[me, i]] * tile, tile), tile)
+            rows = pl.ds(pl.multiple_of(inv[lists_ref[i, me]] * tile, tile), tile)
             dest = pl.ds(pl.multiple_of(i * tile, tile), tile)
             for j in range(slots // 2):
                 block = pair(
                     lambda q: full_ref[rows, pl.ds(pl.multiple_of(q * lanes, lanes), lanes)],
-                    inv[lists_ref[me, 2 * j]],
-                    inv[lists_ref[me, 2 * j + 1]],
+                    inv[lists_ref[2 * j, me]],
+                    inv[lists_ref[2 * j + 1, me]],
                     tile,
                 )
                 slot = 2 * j + lax.broadcasted_iota(jnp.int32, block.shape, 1) // tile
@@ -276,30 +318,28 @@
 
     @pl.when(step == pl.num_programs(0) - 1)
     def _():
-        acc[...] = acc[...] + acc[...].T
-
-        @pl.loop(0, n)
-        def _(r):
-            rows = pl.ds(pl.multiple_of(pos[r] * tile, tile), tile)
+        both = acc[...] + acc[...].T
+        for q in range(funcs // lanes):
+            block = both[:, q * lanes : (q + 1) * lanes]
+            turned[2 * q] = block
+            turned[2 * q + 1] = pltpu.roll(block, tile, 1)
+        low = lax.broadcasted_iota(jnp.int32, (tile, lanes), 1) < tile
+
+        @pl.loop(0, chips)
+        def _(chip):
+            first, second = pos[2 * chip], pos[2 * chip + 1]
+            other = 2 * lax.div(second, 2) + 1 - lax.rem(second, 2)
+            keep = jnp.where(low, has[2 * chip].astype(F32), has[2 * chip + 1].astype(F32))
             for g in range(groups):
-                chip = lax.rem(r // 2 + g, chips)
-                block = pair(
-                    lambda q: acc[rows, pl.ds(pl.multiple_of(q * lanes, lanes), lanes)],
-                    pos[2 * chip],
-                    pos[2 * chip + 1],
-                    tile,
-                )
-                low = lax.broadcasted_iota(jnp.int32, block.shape, 1) < tile
-                keep = jnp.where(
-                    low,
-                    jnp.full(block.shape, has[r] * has[2 * chip], jnp.int32),
-                    jnp.full(block.shape, has[r] * has[2 * chip + 1], jnp.int32),
-                )
-                out_ref[r, g] = jnp.where(keep == 1, block, 0.0)
+                for core in range(2):
+                    r = 2 * lax.rem(chip + chips - g, chips) + core
+                    rows = pl.ds(pl.multiple_of(pos[r] * tile, tile), tile)
+                    block = jnp.where(low, turned[first, rows], turned[other, rows])
+                    out_ref[r, g] = block * (keep * has[r].astype(F32))
 
 
 def reduce_kernel(
-    n, part_ref, line, core_in, side_in, plane_in, msg, got,
+    n, part_ref, inv_ref, out_ref, line, core_in, side_in, plane_in, msg, got,
     core_sem, side_sem, plane_sem, msg_sem,
 ):
     planes, chips = n // 4, n // 2
@@ -321,72 +361,89 @@
 
     pl.semaphore_wait(barrier, n - 1)
 
-    def remote(src, dst, sems, slot, peer):
+    cuts = cut(groups)
+    halves = range(len(cuts) - 1)
+
+    def group(h):
+        return pl.ds(cuts[h], cuts[h + 1] - cuts[h])
+
+    def remote(src, dst, sems, h, slot, peer):
         return pltpu.make_async_remote_copy(
-            src_ref=src, dst_ref=dst, send_sem=sems.at[0, slot], recv_sem=sems.at[1, slot],
+            src_ref=src, dst_ref=dst,
+            send_sem=sems.at[0, h, slot], recv_sem=sems.at[1, h, slot],
             device_id=to(peer), device_id_type=MESH,
         )
 
-    def by_core(zz, side):
+    def by_core(zz, side, h):
         j = zz * 2 + side
-        return remote(part_ref.at[2 * j + 1 - c], core_in.at[j], core_sem, j, core_peer)
-
-    def by_side(zz):
-        return remote(core_in.at[zz * 2 + 1 - y], side_in.at[zz], side_sem, zz, side_peer)
-
-    def by_plane(zz, sign):
+        return remote(
+            part_ref.at[2 * j + 1 - c, group(h)], core_in.at[j, group(h)], core_sem, h, j, core_peer
+        )
+
+    def by_side(zz, h):
+        return remote(
+            core_in.at[zz * 2 + 1 - y, group(h)], side_in.at[zz, group(h)],
+            side_sem, h, zz, side_peer,
+        )
+
+    def by_plane(zz, sign, h):
         way = 0 if sign > 0 else 1
         return remote(
-            side_in.at[zz], plane_in.at[way, zz], plane_sem, way * planes + zz, me + 4 * sign
+            side_in.at[zz, group(h)], plane_in.at[way, zz, group(h)],
+            plane_sem, h, way * planes + zz, me + 4 * sign,
         )
 
     def far_to_near(fn):
         for k in range(planes - 1, -1, -1):
-            for sign in (1, -1):
-                zz = z + sign * k
-                @pl.when((zz >= 0) & (zz < planes))
-                def _():
-                    fn(zz, k, sign)
-                if k == 0:
-                    break
-
-    def start_core(zz, k, sign):
-        by_core(zz, 1 - y).start()
-        by_core(zz, y).start()
+            for h in halves:
+                for sign in (1, -1):
+                    zz = z + sign * k
+                    @pl.when((zz >= 0) & (zz < planes))
+                    def _():
+                        fn(zz, k, sign, h)
+                    if k == 0:
+                        break
+
+    def start_core(zz, k, sign, h):
+        by_core(zz, 1 - y, h).start()
+        by_core(zz, y, h).start()
 
     far_to_near(start_core)
 
-    def side_step(zz, k, sign):
-        by_core(zz, 1 - y).wait_recv()
+    def side_step(zz, k, sign, h):
+        by_core(zz, 1 - y, h).wait_recv()
         j = zz * 2 + 1 - y
-        core_in[j] = core_in[j] + part_ref[2 * j + c]
-        by_side(zz).start()
+        core_in[j, group(h)] = core_in[j, group(h)] + part_ref[2 * j + c, group(h)]
+        by_side(zz, h).start()
 
     far_to_near(side_step)
 
-    def plane_step(zz, k, sign):
-        by_core(zz, y).wait_recv()
+    def plane_step(zz, k, sign, h):
+        by_core(zz, y, h).wait_recv()
         j = zz * 2 + y
-        core_in[j] = core_in[j] + part_ref[2 * j + c]
-        by_side(zz).wait_recv()
-        side_in[zz] = side_in[zz] + core_in[j]
+        by_side(zz, h).wait_recv()
+        total = side_in[zz, group(h)] + (core_in[j, group(h)] + part_ref[2 * j + c, group(h)])
+        side_in[zz, group(h)] = total
         if k:
             behind = (z > 0) if sign > 0 else (z < planes - 1)
 
             @pl.when(behind)
             def _():
-                by_plane(zz, sign).wait_recv()
-                side_in[zz] = side_in[zz] + plane_in[0 if sign > 0 else 1, zz]
-
-            by_plane(zz, sign).start()
+                by_plane(zz, sign, h).wait_recv()
+                way = 0 if sign > 0 else 1
+                side_in[zz, group(h)] = side_in[zz, group(h)] + plane_in[way, zz, group(h)]
+
+            by_plane(zz, sign, h).start()
 
     far_to_near(plane_step)
 
-    for ok, sign in ((z > 0, 1), (z < planes - 1, -1)):
-        @pl.when(ok)
-        def _():
-            by_plane(z, sign).wait_recv()
-            side_in[z] = side_in[z] + plane_in[0 if sign > 0 else 1, z]
+    for h in halves:
+        for ok, sign in ((z > 0, 1), (z < planes - 1, -1)):
+            @pl.when(ok)
+            def _():
+                by_plane(z, sign, h).wait_recv()
+                way = 0 if sign > 0 else 1
+                side_in[z, group(h)] = side_in[z, group(h)] + plane_in[way, z, group(h)]
 
     def by_mirror(i, g, core):
         return pltpu.make_async_remote_copy(
@@ -419,12 +476,18 @@
             wide = got[i, core]
             blocks.append(jnp.concatenate([wide[:, :tile], wide[:, tile:]], axis=0))
         line[lax.rem(chip + chips - g, chips)] = jnp.concatenate(blocks, axis=0).T
-    def sent(zz, k, sign):
-        by_core(zz, y).wait_send()
-        by_core(zz, 1 - y).wait_send()
-        by_side(zz).wait_send()
+    columns = [line[q] for q in range(chips)]
+    for q in range(chips):
+        out_ref[:, q * lanes : (q + 1) * lanes] = chosen(
+            columns, inv_ref[2 * q], inv_ref[2 * q + 1], tile
+        )
+
+    def sent(zz, k, sign, h):
+        by_core(zz, y, h).wait_send()
+        by_core(zz, 1 - y, h).wait_send()
+        by_side(zz, h).wait_send()
         if k:
-            by_plane(zz, sign).wait_send()
+            by_plane(zz, sign, h).wait_send()
 
     far_to_near(sent)
     for i, g in enumerate(mirrored):
@@ -442,29 +505,22 @@
     vmem = pl.BlockSpec(memory_space=pltpu.VMEM)
     smem = pl.BlockSpec(memory_space=pltpu.SMEM)
     dma = pltpu.SemaphoreType.DMA
-    own = pl.pallas_call(
-        functools.partial(pack_kernel, n),
-        out_shape=jax.ShapeDtypeStruct((groups, tile, lanes), F32),
-        in_specs=[vmem, smem],
-        out_specs=vmem,
-        name="pack_density",
-    )(density_slabs, owned_rows)
     full = pl.pallas_call(
         functools.partial(gather_kernel, n),
         out_shape=jax.ShapeDtypeStruct((width, width), F32),
-        in_specs=[vmem],
+        in_specs=[vmem, smem],
         out_specs=vmem,
         scratch_shapes=[
             pltpu.VMEM((n, groups, tile, lanes), F32),
-            dma((4, n)),
-            dma((n,)),
+            dma((PIECES, 4, n)),
+            dma((PIECES, n)),
         ],
         compiler_params=pltpu.CompilerParams(
             collective_id=0, has_side_effects=True, vmem_limit_bytes=VMEM_LIMIT
         ),
         name="gather_density",
-    )(own)
-    chunk = min(npts, 256)
+    )(density_slabs, owned_rows)
+    chunk = min(npts, 2**18 // funcs)
     part, inv = pl.pallas_call(
         functools.partial(compute_kernel, n, groups),
         grid=(npts // chunk,),
@@ -483,6 +539,7 @@
             pltpu.VMEM((funcs, funcs), BF16),
             pltpu.VMEM((funcs, funcs), BF16),
             pltpu.VMEM((funcs, funcs), F32),
+            pltpu.VMEM((funcs // tile, funcs, lanes), F32),
             pltpu.SMEM((n,), jnp.int32),
             pltpu.SMEM((n,), jnp.int32),
             pltpu.SMEM((n,), jnp.int32),
@@ -490,38 +547,32 @@
         compiler_params=pltpu.CompilerParams(vmem_limit_bytes=VMEM_LIMIT),
         name="batch_potential",
     )(
-        full, tile_lists, tile_counts, owned_rows,
+        full, tile_lists.T, tile_counts, owned_rows,
         basis_values, basis_grads, weights.reshape(1, npts),
     )
     mirrored = len([g for g in range(1, groups) if 2 * g != chips])
-    line = pl.pallas_call(
+    return pl.pallas_call(
         functools.partial(reduce_kernel, n),
-        out_shape=jax.ShapeDtypeStruct((chips, tile, lanes), F32),
-        in_specs=[vmem],
+        out_shape=jax.ShapeDtypeStruct((tile, width), F32),
+        in_specs=[vmem, smem],
         out_specs=vmem,
         scratch_shapes=[
+            pltpu.VMEM((chips, tile, lanes), F32),
             pltpu.VMEM((chips, groups, tile, lanes), F32),
             pltpu.VMEM((planes, groups, tile, lanes), F32),
             pltpu.VMEM((2, planes, groups, tile, lanes), F32),
             pltpu.VMEM((mirrored, 2, tile // 2, lanes), F32),
             pltpu.VMEM((mirrored, 2, tile // 2, lanes), F32),
-            dma((2, chips)),
-            dma((2, planes)),
-            dma((2, 2 * planes)),
+            dma((2, PIECES, chips)),
+            dma((2, PIECES, planes)),
+            dma((2, PIECES, 2 * planes)),
             dma((2, 2 * mirrored)),
         ],
         compiler_params=pltpu.CompilerParams(
             collective_id=1, has_side_effects=True, vmem_limit_bytes=VMEM_LIMIT
         ),
         name="reduce_potential",
-    )(part)
-    return pl.pallas_call(
-        order_kernel,
-        out_shape=jax.ShapeDtypeStruct((tile, width), F32),
-        in_specs=[vmem, smem],
-        out_specs=vmem,
-        name="order_columns",
-    )(line, inv)
+    )(part, inv)
 
 
 def solution(mesh):

time: 80.8 us -> 73.3 us (0.907)
  Pallas kernels: 79.2 us -> 71.4 us
    pallas_call x2 -> x0, Pallas kernels: 3.67 us -> none  [the longest x1 1.87 us: shards(): pl.pallas_call(order_kernel, out_shape=jax.ShapeDtypeStruct((tile, width)...]
    pallas_call x1, Pallas kernels: 16.2 us -> 13.8 us  [shards(): pl.pallas_call(functools.partial(compute_kernel, n, groups), grid=(npts /...]
    pallas_call x1, Pallas kernels: 27.8 us -> 26.9 us  [shards(): pl.pallas_call(functools.partial(gather_kernel, n), out_shape=jax.ShapeDt...]
where the time goes in v2:
time: 73.3 us; the launch traced here: 73.1 us
  Pallas kernels  71.4 us (97%)
  local copies, waits for them, and re-layouts  1.67 us (2%)
    pallas_call x1, Pallas kernels, shards(): pl.pallas_call(functools.partial(reduce_kernel, n), out_shape=jax.ShapeDt...  30.7 us
    pallas_call x1, Pallas kernels, shards(): pl.pallas_call(functools.partial(gather_kernel, n), out_shape=jax.ShapeDt...  26.9 us
    pallas_call x1, Pallas kernels, shards(): pl.pallas_call(functools.partial(compute_kernel, n, groups), grid=(npts /...  13.8 us
    unnamed x1, local copies, waits for them, and re-layouts  1.67 us

profile of v2, /device:TPU:0, one launch (start us, length us, event | category | flops | bytes accessed | tf_op | source)
XLA Modules:
  0.0 73.1 jit_solution(12234886607757869272)
XLA Ops:
  0.0 26.9 %gather_density.1.full_ref = f32[1024,1024]{1,0:T(8,128)} custom-call(f32[64,1024]{1,0:T(8,128)} %slab_ref.1, s32[16]{0:T(128)} %owned_ref.3), custom_call_target="tpu_custom_call" | custom-call | tf_op jit(solution)/shard_map/gather_density/pallas_call | solution.py:508
  26.9 13.8 %batch_potential.1 = (f32[16,5,64,128]{3,2,1,0:T(8,128)}, s32[16]{0:T(128)}) custom-call(f32[1024,1024]{1,0:T(8,128)} %gather_density.1.full_ref, s32[8,16]{1,0:T(8,128)} %bitcast.2, s32[16]{0:T(128)} %counts_ref.1, s32[16]{0:T(128)} %owned_ref.3, f32[1024,512]{1,0:T(8,128)} %phi_ref.1, f32[3,1024,512]{2,1,0:T(8,128)} %grad_ref.1, f32[1,1024]{1,0:T(1,128)} %bitcast.3), custom_call_target="tpu_custom_call" | custom-call | tf_op jit(solution)/shard_map/batch_potential/pallas_call | solution.py:524
  40.7 30.7 %reduce_potential.1 = f32[64,1024]{1,0:T(8,128)} custom-call(f32[16,5,64,128]{3,2,1,0:T(8,128)} %get-tuple-element.7.part_ref, s32[16]{0:T(128)} %get-tuple-element.8.inv_ref), custom_call_target="tpu_custom_call" | custom-call | tf_op jit(solution)/shard_map/reduce_potential/pallas_call | solution.py:554
  71.4 1.7 %copy.9 = f32[64,1024]{1,0:T(8,128)} copy(f32[64,1024]{1,0:T(8,128)} %reduce_potential.1) | data formatting | bytes 524288

commit v3 on v2

--- a/solution.py
+++ b/solution.py
@@ -339,11 +339,11 @@
 
 
 def reduce_kernel(
-    n, part_ref, inv_ref, out_ref, line, core_in, side_in, plane_in, msg, got,
-    core_sem, side_sem, plane_sem, msg_sem,
+    n, part_ref, inv_ref, out_ref, line, core_in, side_in, plane_in, msg, got, held,
+    core_sem, side_sem, plane_sem, msg_sem, held_sem,
 ):
     planes, chips = n // 4, n // 2
-    groups, tile = part_ref.shape[1], part_ref.shape[2]
+    groups, tile = held.shape[1], held.shape[2]
     lanes = 2 * tile
     half = tile // 2
     me, z, y, c = place(n)
@@ -351,6 +351,9 @@
     chip = me // 2
     mirrored = [g for g in range(1, groups) if 2 * g != chips]
 
+    def fetch(j):
+        return pltpu.make_async_copy(part_ref.at[2 * j + c], held.at[j], held_sem.at[j])
+
     barrier = pltpu.get_barrier_semaphore()
 
     @pl.loop(1, n)
@@ -359,6 +362,8 @@
             barrier, inc=1, device_id=to(lax.rem(me + k, n)), device_id_type=MESH
         )
 
+    for j in range(chips):
+        fetch(j).start()
     pl.semaphore_wait(barrier, n - 1)
 
     cuts = cut(groups)
@@ -409,11 +414,13 @@
         by_core(zz, y, h).start()
 
     far_to_near(start_core)
+    for j in range(chips):
+        fetch(j).wait()
 
     def side_step(zz, k, sign, h):
         by_core(zz, 1 - y, h).wait_recv()
         j = zz * 2 + 1 - y
-        core_in[j, group(h)] = core_in[j, group(h)] + part_ref[2 * j + c, group(h)]
+        core_in[j, group(h)] = core_in[j, group(h)] + held[j, group(h)]
         by_side(zz, h).start()
 
     far_to_near(side_step)
@@ -422,7 +429,7 @@
         by_core(zz, y, h).wait_recv()
         j = zz * 2 + y
         by_side(zz, h).wait_recv()
-        total = side_in[zz, group(h)] + (core_in[j, group(h)] + part_ref[2 * j + c, group(h)])
+        total = side_in[zz, group(h)] + (core_in[j, group(h)] + held[j, group(h)])
         side_in[zz, group(h)] = total
         if k:
             behind = (z > 0) if sign > 0 else (z < planes - 1)
@@ -436,14 +443,6 @@
             by_plane(zz, sign, h).start()
 
     far_to_near(plane_step)
-
-    for h in halves:
-        for ok, sign in ((z > 0, 1), (z < planes - 1, -1)):
-            @pl.when(ok)
-            def _():
-                by_plane(z, sign, h).wait_recv()
-                way = 0 if sign > 0 else 1
-                side_in[z, group(h)] = side_in[z, group(h)] + plane_in[way, z, group(h)]
 
     def by_mirror(i, g, core):
         return pltpu.make_async_remote_copy(
@@ -455,11 +454,20 @@
             device_id_type=MESH,
         )
 
-    for i, g in enumerate(mirrored):
-        for core in range(2):
-            block = side_in[z, g, :, core * tile : (core + 1) * tile]
-            msg[i, core] = jnp.concatenate([block[:half], block[half:]], axis=1)
-            by_mirror(i, g, core).start()
+    for h in halves:
+        for ok, sign in ((z > 0, 1), (z < planes - 1, -1)):
+            @pl.when(ok)
+            def _():
+                by_plane(z, sign, h).wait_recv()
+                way = 0 if sign > 0 else 1
+                side_in[z, group(h)] = side_in[z, group(h)] + plane_in[way, z, group(h)]
+
+        for i, g in enumerate(mirrored):
+            if cuts[h] <= g < cuts[h + 1]:
+                for core in range(2):
+                    block = side_in[z, g, :, core * tile : (core + 1) * tile]
+                    msg[i, core] = jnp.concatenate([block[:half], block[half:]], axis=1)
+                    by_mirror(i, g, core).start()
     for g in range(groups):
         line[lax.rem(chip + g, chips)] = side_in[z, g]
     for i, g in enumerate(mirrored):
@@ -554,7 +562,7 @@
     return pl.pallas_call(
         functools.partial(reduce_kernel, n),
         out_shape=jax.ShapeDtypeStruct((tile, width), F32),
-        in_specs=[vmem, smem],
+        in_specs=[pl.BlockSpec(memory_space=pl.ANY), smem],
         out_specs=vmem,
         scratch_shapes=[
             pltpu.VMEM((chips, tile, lanes), F32),
@@ -563,10 +571,12 @@
             pltpu.VMEM((2, planes, groups, tile, lanes), F32),
             pltpu.VMEM((mirrored, 2, tile // 2, lanes), F32),
             pltpu.VMEM((mirrored, 2, tile // 2, lanes), F32),
+            pltpu.VMEM((chips, groups, tile, lanes), F32),
             dma((2, PIECES, chips)),
             dma((2, PIECES, planes)),
             dma((2, PIECES, 2 * planes)),
             dma((2, 2 * mirrored)),
+            dma((chips,)),
         ],
         compiler_params=pltpu.CompilerParams(
             collective_id=1, has_side_effects=True, vmem_limit_bytes=VMEM_LIMIT

time: 73.3 us -> 72.2 us (0.985)
  Pallas kernels: 71.4 us -> 70.3 us
    pallas_call x1, Pallas kernels: 30.7 us -> 29.6 us  [shards(): pl.pallas_call(functools.partial(reduce_kernel, n), out_shape=jax.ShapeDt...]
where the time goes in v3:
time: 72.2 us; the launch traced here: 72 us
  Pallas kernels  70.3 us (97%)
  local copies, waits for them, and re-layouts  1.67 us (2%)
    pallas_call x1, Pallas kernels, shards(): pl.pallas_call(functools.partial(reduce_kernel, n), out_shape=jax.ShapeDt...  29.6 us
    pallas_call x1, Pallas kernels, shards(): pl.pallas_call(functools.partial(gather_kernel, n), out_shape=jax.ShapeDt...  26.9 us
    pallas_call x1, Pallas kernels, shards(): pl.pallas_call(functools.partial(compute_kernel, n, groups), grid=(npts /...  13.8 us
    unnamed x1, local copies, waits for them, and re-layouts  1.67 us

profile of v3, /device:TPU:0, one launch (start us, length us, event | category | flops | bytes accessed | tf_op | source)
XLA Modules:
  0.0 72.0 jit_solution(7753851925428460313)
XLA Ops:
  0.0 26.9 %gather_density.1.full_ref = f32[1024,1024]{1,0:T(8,128)} custom-call(f32[64,1024]{1,0:T(8,128)} %slab_ref.1, s32[16]{0:T(128)} %owned_ref.3), custom_call_target="tpu_custom_call" | custom-call | tf_op jit(solution)/shard_map/gather_density/pallas_call | solution.py:516
  26.9 13.8 %batch_potential.1 = (f32[16,5,64,128]{3,2,1,0:T(8,128)}, s32[16]{0:T(128)}) custom-call(f32[1024,1024]{1,0:T(8,128)} %gather_density.1.full_ref, s32[8,16]{1,0:T(8,128)} %bitcast.2, s32[16]{0:T(128)} %counts_ref.1, s32[16]{0:T(128)} %owned_ref.3, f32[1024,512]{1,0:T(8,128)} %phi_ref.1, f32[3,1024,512]{2,1,0:T(8,128)} %grad_ref.1, f32[1,1024]{1,0:T(1,128)} %bitcast.3), custom_call_target="tpu_custom_call" | custom-call | tf_op jit(solution)/shard_map/batch_potential/pallas_call | solution.py:532
  40.7 29.6 %reduce_potential.1 = f32[64,1024]{1,0:T(8,128)} custom-call(f32[16,5,64,128]{3,2,1,0:T(8,128)} %get-tuple-element.7.part_ref, s32[16]{0:T(128)} %get-tuple-element.8.inv_ref), custom_call_target="tpu_custom_call" | custom-call | tf_op jit(solution)/shard_map/reduce_potential/pallas_call | solution.py:562
  70.4 1.7 %copy.9 = f32[64,1024]{1,0:T(8,128)} copy(f32[64,1024]{1,0:T(8,128)} %reduce_potential.1) | data formatting | bytes 524288
